TPU v7x, 128 devices: a whole 4x4x4 slice. The times are simulated.
128 devices in a mesh: hi: 16 (over z, x), lo: 8 (over y, core).
Axes of the slice: x: 4, y: 4, z: 4, core: 2. Of those that a mesh axis runs over, the one named last changes fastest.
Arguments:
- sources: bfloat16 [64, 2097152], P(None, ('hi', 'lo')), may hold values from -6 to 6
- leaf_in: bfloat16 [8192, 64, 256], P(('hi', 'lo')), may hold values from -0.375 to 0.375
- local_mix: bfloat16 [8192, 6, 64, 128], P(('hi', 'lo')), may hold values from -0.5 to 0.5
- lo_mix: bfloat16 [8192, 3, 64, 128], P(('hi', 'lo')), may hold values from -0.5 to 0.5
- hi_mix: bfloat16 [8192, 4, 64, 128], P(('hi', 'lo')), may hold values from -0.5 to 0.5
- leaf_out: bfloat16 [8192, 64, 256], P(('hi', 'lo')), may hold values from -0.75 to 0.75
Outputs:
- targets: bfloat16 [64, 2097152], P(None, ('hi', 'lo'))
All inputs are finite; a program needn't handle non-finite values.
Results may differ from a plain program's by a relative error of at most 0.029.
Values may be sent and summed in bfloat16 or wider, within the bound.
A program may use at most 128 MiB of HBM per device.

v0:
```python
import jax
import jax.numpy as jnp
from jax import lax
from jax.sharding import PartitionSpec as P


def swapped(block, axis, stride):
    count = lax.axis_size(axis)
    route = []
    for low in range(count):
        high = low | 1 << stride
        if high != low and high < count:
            route += [(low, high), (high, low)]
    return lax.ppermute(block, axis, route)


def flip_blocks(current, level_bit, block_dim):
    shape_now = current.shape
    head_shape = shape_now[:block_dim]
    grouped = current.reshape(
        head_shape
        + (shape_now[block_dim] >> level_bit + 1, 2, 1 << level_bit)
        + shape_now[block_dim + 1 :]
    )
    return lax.rev(grouped, (block_dim + 1,)).reshape(shape_now)


def mix_level(current, partner, factors):
    joined = jnp.concatenate([current, partner], axis=-1)
    mixed = jnp.einsum("kvs,kqs->kvq", joined, factors, preferred_element_type=jnp.float32)
    return mixed.astype(jnp.bfloat16)


def body(sources, leaf_in, local_mix, lo_mix, hi_mix, leaf_out):
    blocks_here = leaf_in.shape[0]
    leaf_size = leaf_in.shape[2]
    vectors = sources.shape[0]
    local_levels = local_mix.shape[1]
    lo_count = lax.axis_size("lo")
    lo_levels = lo_count.bit_length() - 1
    hi_levels = lax.axis_size("hi").bit_length() - 1
    source_blocks = sources.reshape(vectors, blocks_here, leaf_size)
    current = jnp.einsum(
        "vkl,krl->kvr", source_blocks, leaf_in, preferred_element_type=jnp.float32
    ).astype(jnp.bfloat16)
    for level in range(local_levels):
        current = mix_level(current, flip_blocks(current, level, 0), local_mix[:, level])
    for level in range(lo_levels):
        partner = swapped(current, "lo", level)
        current = mix_level(current, partner, lo_mix[:, level])
    for level in range(hi_levels):
        partner = swapped(current, "hi", level)
        current = mix_level(current, partner, hi_mix[:, level])
    result = jnp.einsum("kvr,krl->vkl", current, leaf_out, preferred_element_type=jnp.float32)
    return result.reshape(vectors, blocks_here * leaf_size).astype(jnp.bfloat16)


def solution(mesh):
    return jax.shard_map(
        body,
        mesh=mesh,
        in_specs=(
            P(None, ("hi", "lo")),
            P(("hi", "lo"), None, None),
            P(("hi", "lo"), None, None, None),
            P(("hi", "lo"), None, None, None),
            P(("hi", "lo"), None, None, None),
            P(("hi", "lo"), None, None),
        ),
        out_specs=P(None, ("hi", "lo")),
        check_vma=False,
    )
```

profile of v0, /device:TPU:0, one launch (start us, length us, event | category | flops | bytes accessed | tf_op | source)
XLA Modules:
  0.0 195.3 jit_solution(407974088822866719)
XLA Ops:
  0.0 3.1 %fusion.3 = bf16[64,64,64]{2,1,0:T(8,128)(2,1)S(1)} fusion(bf16[64,64,256]{2,1,0:T(8,128)(2,1)} %param.7, bf16[8,64,8,256]{3,2,1,0:T(8,128)(2,1)} %bitcast.100), kind=kOutput, calls=%fused_computation.4 | convolution fusion | flops 134479872 | bytes 4718592 | tf_op jit(solution)/shard_map/vkl,krl->kvr/dot_general | solution.py:43
  4.2 3.3 %convolution_convert_fusion.12 = bf16[64,64,64]{2,1,0:T(8,128)(2,1)} fusion(bf16[64,64,64]{2,1,0:T(8,128)(2,1)} %bitcast.94, bf16[64,64,64]{2,1,0:T(8,128)(2,1)S(1)} %fusion.3, bf16[64,6,64,128]{3,2,1,0:T(8,128)(2,1)} %param.8), kind=kOutput, calls=%fused_computation.17 | convolution fusion | flops 69468160 | bytes 3145728 | tf_op jit(solution)/shard_map/kvs,kqs->kvq/dot_general | solution.py:30
  7.4 2.4 %rev.19 = bf16[16,2,2,64,64]{4,3,2,1,0:T(8,128)(2,1)} reverse(bf16[16,2,2,64,64]{4,3,2,1,0:T(8,128)(2,1)} %bitcast.89), dimensions={1} | reverse | bytes 1048576 | tf_op jit(solution)/shard_map/rev | solution.py:25
  9.8 3.3 %convolution_convert_fusion.11 = bf16[64,64,64]{2,1,0:T(8,128)(2,1)} fusion(bf16[64,64,64]{2,1,0:T(8,128)(2,1)} %bitcast.95, bf16[64,64,64]{2,1,0:T(8,128)(2,1)S(1)} %copy-done.1, bf16[64,6,64,128]{3,2,1,0:T(8,128)(2,1)} %param.8), kind=kOutput, calls=%fused_computation.16 | convolution fusion | flops 69468160 | bytes 3145728 | tf_op jit(solution)/shard_map/kvs,kqs->kvq/dot_general | solution.py:30
  13.1 2.4 %rev.20 = bf16[8,2,4,64,64]{4,3,2,1,0:T(8,128)(2,1)} reverse(bf16[8,2,4,64,64]{4,3,2,1,0:T(8,128)(2,1)} %bitcast.90), dimensions={1} | reverse | bytes 1048576 | tf_op jit(solution)/shard_map/rev | solution.py:25
  15.5 3.3 %convolution_convert_fusion.10 = bf16[64,64,64]{2,1,0:T(8,128)(2,1)} fusion(bf16[64,64,64]{2,1,0:T(8,128)(2,1)} %bitcast.96, bf16[64,64,64]{2,1,0:T(8,128)(2,1)S(1)} %copy-done.2, bf16[64,6,64,128]{3,2,1,0:T(8,128)(2,1)} %param.8), kind=kOutput, calls=%fused_computation.15 | convolution fusion | flops 69468160 | bytes 3145728 | tf_op jit(solution)/shard_map/kvs,kqs->kvq/dot_general | solution.py:30
  18.8 2.4 %rev.21 = bf16[4,2,8,64,64]{4,3,2,1,0:T(8,128)(2,1)} reverse(bf16[4,2,8,64,64]{4,3,2,1,0:T(8,128)(2,1)} %bitcast.91), dimensions={1} | reverse | bytes 1048576 | tf_op jit(solution)/shard_map/rev | solution.py:25
  21.1 3.3 %convolution_convert_fusion.9 = bf16[64,64,64]{2,1,0:T(8,128)(2,1)} fusion(bf16[64,64,64]{2,1,0:T(8,128)(2,1)} %bitcast.97, bf16[64,64,64]{2,1,0:T(8,128)(2,1)S(1)} %copy-done.3, bf16[64,6,64,128]{3,2,1,0:T(8,128)(2,1)} %param.8), kind=kOutput, calls=%fused_computation.14 | convolution fusion | flops 69468160 | bytes 3145728 | tf_op jit(solution)/shard_map/kvs,kqs->kvq/dot_general | solution.py:30
  24.4 2.4 %rev.22 = bf16[2,2,16,64,64]{4,3,2,1,0:T(8,128)(2,1)} reverse(bf16[2,2,16,64,64]{4,3,2,1,0:T(8,128)(2,1)} %bitcast.92), dimensions={1} | reverse | bytes 1048576 | tf_op jit(solution)/shard_map/rev | solution.py:25
  26.7 3.3 %convolution_convert_fusion.8 = bf16[64,64,64]{2,1,0:T(8,128)(2,1)} fusion(bf16[64,64,64]{2,1,0:T(8,128)(2,1)} %bitcast.98, bf16[64,64,64]{2,1,0:T(8,128)(2,1)S(1)} %copy-done.4, bf16[64,6,64,128]{3,2,1,0:T(8,128)(2,1)} %param.8), kind=kOutput, calls=%fused_computation.13 | convolution fusion | flops 69468160 | bytes 3145728 | tf_op jit(solution)/shard_map/kvs,kqs->kvq/dot_general | solution.py:30
  30.0 2.4 %rev.23 = bf16[1,2,32,64,64]{4,3,2,1,0:T(8,128)(2,1)} reverse(bf16[1,2,32,64,64]{4,3,2,1,0:T(8,128)(2,1)} %bitcast.93), dimensions={1} | reverse | bytes 1048576 | tf_op jit(solution)/shard_map/rev | solution.py:25
  32.4 2.4 %convolution_convert_fusion.7 = bf16[64,64,64]{2,1,0:T(8,128)(2,1)S(1)} fusion(bf16[64,64,64]{2,1,0:T(8,128)(2,1)} %bitcast.99, bf16[64,64,64]{2,1,0:T(8,128)(2,1)S(1)} %copy-done.5, bf16[64,6,64,128]{3,2,1,0:T(8,128)(2,1)} %param.8), kind=kOutput, calls=%fused_computation.12 | convolution fusion | flops 69468160 | bytes 3145728 | tf_op jit(solution)/shard_map/kvs,kqs->kvq/dot_general | solution.py:30
  34.9 2.6 %collective-permute-done = bf16[64,64,64]{2,1,0:T(8,128)(2,1)S(1)} collective-permute-done((bf16[64,64,64]{2,1,0:T(8,128)(2,1)S(1)}, bf16[64,64,64]{2,1,0:T(8,128)(2,1)S(1)}, u32[]{:S(2)}, u32[]{:S(2)}) %collective-permute-start) | collective-permute-done | bytes 524320 | tf_op jit(solution)/shard_map/ppermute | solution.py:14
  40.1 23.5 %collective-permute-done.1 = bf16[64,64,64]{2,1,0:T(8,128)(2,1)S(1)} collective-permute-done((bf16[64,64,64]{2,1,0:T(8,128)(2,1)S(1)}, bf16[64,64,64]{2,1,0:T(8,128)(2,1)S(1)}, u32[]{:S(2)}, u32[]{:S(2)}) %collective-permute-start.1) | collective-permute-done | bytes 524320 | tf_op jit(solution)/shard_map/ppermute | solution.py:14
  64.4 3.4 %collective-permute-start.2 = (bf16[64,64,64]{2,1,0:T(8,128)(2,1)S(1)}, bf16[64,64,64]{2,1,0:T(8,128)(2,1)S(1)}, u32[]{:S(2)}, u32[]{:S(2)}) collective-permute-start(bf16[64,64,64]{2,1,0:T(8,128)(2,1)S(1)} %convolution_convert_fusion.5), channel_id=1, source_target_pairs={{0,4},{4,0},{1,5},{5,1},{2,6},{6,2},{3,7},{7,3},{8,12},{12,8},{9,1... | collective-permute-start | bytes 1572872 | tf_op jit(solution)/shard_map/ppermute | solution.py:14
  67.7 22.6 %collective-permute-done.2 = bf16[64,64,64]{2,1,0:T(8,128)(2,1)S(1)} collective-permute-done((bf16[64,64,64]{2,1,0:T(8,128)(2,1)S(1)}, bf16[64,64,64]{2,1,0:T(8,128)(2,1)S(1)}, u32[]{:S(2)}, u32[]{:S(2)}) %collective-permute-start.2) | collective-permute-done | bytes 524320 | tf_op jit(solution)/shard_map/ppermute | solution.py:14
  92.7 21.9 %collective-permute-done.3 = bf16[64,64,64]{2,1,0:T(8,128)(2,1)S(1)} collective-permute-done((bf16[64,64,64]{2,1,0:T(8,128)(2,1)S(1)}, bf16[64,64,64]{2,1,0:T(8,128)(2,1)S(1)}, u32[]{:S(2)}, u32[]{:S(2)}) %collective-permute-start.3) | collective-permute-done | bytes 524320 | tf_op jit(solution)/shard_map/ppermute | solution.py:14
  115.4 3.1 %collective-permute-start.4 = (bf16[64,64,64]{2,1,0:T(8,128)(2,1)S(1)}, bf16[64,64,64]{2,1,0:T(8,128)(2,1)S(1)}, u32[]{:S(2)}, u32[]{:S(2)}) collective-permute-start(bf16[64,64,64]{2,1,0:T(8,128)(2,1)S(1)} %convolution_convert_fusion.3), channel_id=1, source_target_pairs={{0,16},{16,0},{8,24},{24,8},{32,48},{48,32},{40,56},{56,40},{64,80... | collective-permute-start | bytes 1572872 | tf_op jit(solution)/shard_map/ppermute | solution.py:14
  118.5 21.0 %collective-permute-done.4 = bf16[64,64,64]{2,1,0:T(8,128)(2,1)S(1)} collective-permute-done((bf16[64,64,64]{2,1,0:T(8,128)(2,1)S(1)}, bf16[64,64,64]{2,1,0:T(8,128)(2,1)S(1)}, u32[]{:S(2)}, u32[]{:S(2)}) %collective-permute-start.4) | collective-permute-done | bytes 524320 | tf_op jit(solution)/shard_map/ppermute | solution.py:14
  142.3 19.9 %collective-permute-done.5 = bf16[64,64,64]{2,1,0:T(8,128)(2,1)S(1)} collective-permute-done((bf16[64,64,64]{2,1,0:T(8,128)(2,1)S(1)}, bf16[64,64,64]{2,1,0:T(8,128)(2,1)S(1)}, u32[]{:S(2)}, u32[]{:S(2)}) %collective-permute-start.5) | collective-permute-done | bytes 524320 | tf_op jit(solution)/shard_map/ppermute | solution.py:14
  162.9 5.2 %collective-permute-start.6 = (bf16[64,64,64]{2,1,0:T(8,128)(2,1)S(1)}, bf16[64,64,64]{2,1,0:T(8,128)(2,1)}, u32[]{:S(2)}, u32[]{:S(2)}) collective-permute-start(bf16[64,64,64]{2,1,0:T(8,128)(2,1)S(1)} %convolution_convert_fusion.1), channel_id=1, source_target_pairs={{0,64},{64,0},{8,72},{72,8},{16,80},{80,16},{24,88},{88,24},{32,96... | collective-permute-start | bytes 1572872 | tf_op jit(solution)/shard_map/ppermute | solution.py:14
  168.0 20.0 %collective-permute-done.6 = bf16[64,64,64]{2,1,0:T(8,128)(2,1)} collective-permute-done((bf16[64,64,64]{2,1,0:T(8,128)(2,1)S(1)}, bf16[64,64,64]{2,1,0:T(8,128)(2,1)}, u32[]{:S(2)}, u32[]{:S(2)}) %collective-permute-start.6) | collective-permute-done | bytes 524320 | tf_op jit(solution)/shard_map/ppermute | solution.py:14
  188.0 4.2 %convert_bitcast_fusion = bf16[64,8,8,256]{3,2,1,0:T(8,128)(2,1)} fusion(bf16[64,64,256]{2,1,0:T(8,128)(2,1)S(1)} %copy-done, bf16[64,64,64]{2,1,0:T(8,128)(2,1)} %collective-permute-done.6, bf16[64,64,64]{2,1,0:T(8,128)(2,1)S(1)} %convolution_convert_fusion.1, bf16[64,4,64,128]{3,2,1,0:T(8,128)(2,1)} %param.10), kind=kOutput, calls=%fused_computation.3 | convolution fusion | flops 204734464 | bytes 6815744 | tf_op jit(solution)/shard_map/kvr,krl->vkl/dot_general | solution.py:54
  192.2 3.0 %copy.47 = bf16[64,8,8,256]{3,2,0,1:T(8,128)(2,1)} copy(bf16[64,8,8,256]{3,2,1,0:T(8,128)(2,1)} %convert_bitcast_fusion) | data formatting | bytes 4194304 | tf_op jit(solution)/shard_map/convert_element_type | solution.py:55
  (27 shorter events, 11.0 us)
Async XLA Ops:
  0.0 188.0 %copy-start = (bf16[64,64,256]{2,1,0:T(8,128)(2,1)S(1)}, bf16[64,64,256]{2,1,0:T(8,128)(2,1)}, u32[]{:S(2)}) copy-start(bf16[64,64,256]{2,1,0:T(8,128)(2,1)} %param.11) | copy-start | bytes 6291460
  7.4 2.4 %copy-start.1 = (bf16[64,64,64]{2,1,0:T(8,128)(2,1)S(1)}, bf16[64,64,64]{2,1,0:T(8,128)(2,1)}, u32[]{:S(2)}) copy-start(bf16[64,64,64]{2,1,0:T(8,128)(2,1)} %convolution_convert_fusion.12) | copy-start | bytes 1572868
  13.1 2.4 %copy-start.2 = (bf16[64,64,64]{2,1,0:T(8,128)(2,1)S(1)}, bf16[64,64,64]{2,1,0:T(8,128)(2,1)}, u32[]{:S(2)}) copy-start(bf16[64,64,64]{2,1,0:T(8,128)(2,1)} %convolution_convert_fusion.11) | copy-start | bytes 1572868
  18.8 2.4 %copy-start.3 = (bf16[64,64,64]{2,1,0:T(8,128)(2,1)S(1)}, bf16[64,64,64]{2,1,0:T(8,128)(2,1)}, u32[]{:S(2)}) copy-start(bf16[64,64,64]{2,1,0:T(8,128)(2,1)} %convolution_convert_fusion.10) | copy-start | bytes 1572868
  24.4 2.4 %copy-start.4 = (bf16[64,64,64]{2,1,0:T(8,128)(2,1)S(1)}, bf16[64,64,64]{2,1,0:T(8,128)(2,1)}, u32[]{:S(2)}) copy-start(bf16[64,64,64]{2,1,0:T(8,128)(2,1)} %convolution_convert_fusion.9) | copy-start | bytes 1572868
  30.0 2.4 %copy-start.5 = (bf16[64,64,64]{2,1,0:T(8,128)(2,1)S(1)}, bf16[64,64,64]{2,1,0:T(8,128)(2,1)}, u32[]{:S(2)}) copy-start(bf16[64,64,64]{2,1,0:T(8,128)(2,1)} %convolution_convert_fusion.8) | copy-start | bytes 1572868
  32.4 5.2 %copy-start.7 = (bf16[64,3,64,128]{3,2,1,0:T(8,128)(2,1)S(1)}, bf16[64,3,64,128]{3,2,1,0:T(8,128)(2,1)}, u32[]{:S(2)}) copy-start(bf16[64,3,64,128]{3,2,1,0:T(8,128)(2,1)} %param.9) | copy-start | bytes 9437188
  34.8 2.7 %collective-permute-start = (bf16[64,64,64]{2,1,0:T(8,128)(2,1)S(1)}, bf16[64,64,64]{2,1,0:T(8,128)(2,1)S(1)}, u32[]{:S(2)}, u32[]{:S(2)}) collective-permute-start(bf16[64,64,64]{2,1,0:T(8,128)(2,1)S(1)} %convolution_convert_fusion.7), channel_id=1, source_target_pairs={{0,1},{1,0},{2,3},{3,2},{4,5},{5,4},{6,7},{7,6},{8,9},{9,8},{10,11... | collective-permute-start | bytes 1572872 | tf_op jit(solution)/shard_map/ppermute | solution.py:14
  38.3 25.3 %collective-permute-start.1 = (bf16[64,64,64]{2,1,0:T(8,128)(2,1)S(1)}, bf16[64,64,64]{2,1,0:T(8,128)(2,1)S(1)}, u32[]{:S(2)}, u32[]{:S(2)}) collective-permute-start(bf16[64,64,64]{2,1,0:T(8,128)(2,1)S(1)} %convolution_convert_fusion.6), channel_id=1, source_target_pairs={{0,2},{2,0},{1,3},{3,1},{4,6},{6,4},{5,7},{7,5},{8,10},{10,8},{9,1... | collective-permute-start | bytes 1572872 | tf_op jit(solution)/shard_map/ppermute | solution.py:14
  64.3 50.3 %copy-start.6 = (bf16[64,4,64,128]{3,2,1,0:T(8,128)(2,1)S(1)}, bf16[64,4,64,128]{3,2,1,0:T(8,128)(2,1)}, u32[]{:S(2)}) copy-start(bf16[64,4,64,128]{3,2,1,0:T(8,128)(2,1)} %param.10) | copy-start | bytes 12582916
  64.4 26.0 %collective-permute-start.2 = (bf16[64,64,64]{2,1,0:T(8,128)(2,1)S(1)}, bf16[64,64,64]{2,1,0:T(8,128)(2,1)S(1)}, u32[]{:S(2)}, u32[]{:S(2)}) collective-permute-start(bf16[64,64,64]{2,1,0:T(8,128)(2,1)S(1)} %convolution_convert_fusion.5), channel_id=1, source_target_pairs={{0,4},{4,0},{1,5},{5,1},{2,6},{6,2},{3,7},{7,3},{8,12},{12,8},{9,1... | collective-permute-start | bytes 1572872 | tf_op jit(solution)/shard_map/ppermute | solution.py:14
  91.1 23.6 %collective-permute-start.3 = (bf16[64,64,64]{2,1,0:T(8,128)(2,1)S(1)}, bf16[64,64,64]{2,1,0:T(8,128)(2,1)S(1)}, u32[]{:S(2)}, u32[]{:S(2)}) collective-permute-start(bf16[64,64,64]{2,1,0:T(8,128)(2,1)S(1)} %convolution_convert_fusion.4), channel_id=1, source_target_pairs={{0,8},{8,0},{16,24},{24,16},{32,40},{40,32},{48,56},{56,48},{64,72... | collective-permute-start | bytes 1572872 | tf_op jit(solution)/shard_map/ppermute | solution.py:14
  115.4 24.1 %collective-permute-start.4 = (bf16[64,64,64]{2,1,0:T(8,128)(2,1)S(1)}, bf16[64,64,64]{2,1,0:T(8,128)(2,1)S(1)}, u32[]{:S(2)}, u32[]{:S(2)}) collective-permute-start(bf16[64,64,64]{2,1,0:T(8,128)(2,1)S(1)} %convolution_convert_fusion.3), channel_id=1, source_target_pairs={{0,16},{16,0},{8,24},{24,8},{32,48},{48,32},{40,56},{56,40},{64,80... | collective-permute-start | bytes 1572872 | tf_op jit(solution)/shard_map/ppermute | solution.py:14
  140.3 21.8 %collective-permute-start.5 = (bf16[64,64,64]{2,1,0:T(8,128)(2,1)S(1)}, bf16[64,64,64]{2,1,0:T(8,128)(2,1)S(1)}, u32[]{:S(2)}, u32[]{:S(2)}) collective-permute-start(bf16[64,64,64]{2,1,0:T(8,128)(2,1)S(1)} %convolution_convert_fusion.2), channel_id=1, source_target_pairs={{0,32},{32,0},{8,40},{40,8},{16,48},{48,16},{24,56},{56,24},{64,96... | collective-permute-start | bytes 1572872 | tf_op jit(solution)/shard_map/ppermute | solution.py:14
  162.9 25.1 %collective-permute-start.6 = (bf16[64,64,64]{2,1,0:T(8,128)(2,1)S(1)}, bf16[64,64,64]{2,1,0:T(8,128)(2,1)}, u32[]{:S(2)}, u32[]{:S(2)}) collective-permute-start(bf16[64,64,64]{2,1,0:T(8,128)(2,1)S(1)} %convolution_convert_fusion.1), channel_id=1, source_target_pairs={{0,64},{64,0},{8,72},{72,8},{16,80},{80,16},{24,88},{88,24},{32,96... | collective-permute-start | bytes 1572872 | tf_op jit(solution)/shard_map/ppermute | solution.py:14
where the time goes:
time: 196 us; the launch traced here: 195 us
  waiting for transfers between devices  132 us (67%)
  matrix products  30.5 us (16%)
  starting transfers between devices  17 us (9%)
  local copies, waits for them, and re-layouts  16 us (8%)
    ppermute x7, waiting for transfers between devices, swapped(): return lax.ppermute(block, axis, route)  132 us
    dot_general x12, matrix products, mix_level(): jnp.einsum('kvs,kqs->kvq', joined, factors, preferred_element_type=jnp.fl...  23.3 us
    ppermute x7, starting transfers between devices, swapped(): return lax.ppermute(block, axis, route)  17 us
    rev x6, local copies, waits for them, and re-layouts, flip_blocks(): return lax.rev(grouped, (block_dim + 1,)).reshape(shape_now)  12.9 us
    dot_general x1, matrix products, body(): jnp.einsum('kvr,krl->vkl', current, leaf_out, preferred_element_type=jnp....  4.18 us
  transfers between devices with their start and end apart: 7, of which 7 were waited for; matrix products, arithmetic and copies ran while one was open for 0% of the time, Pallas kernels for 0%

commit v1 on v0

v1 whole, which is shorter than its diff:
```python
import functools

import jax
import jax.numpy as jnp
from jax import lax
from jax.experimental import pallas as pl
from jax.experimental.pallas import tpu as pltpu
from jax.sharding import PartitionSpec as P

MESH = pl.DeviceIdType.MESH
GROUP = 1
OFFSETS = (0, 2, 5, 8, 11, 14, 17, 20)
CHUNKS = 4
UNROLL = 4


def low_lanes(shape):
    return lax.broadcasted_iota(jnp.int32, shape, len(shape) - 1) < shape[-1] // 2


def mixed(own, partner, f_low, f_high):
    zero = jnp.zeros_like(own)
    low = low_lanes(own.shape)
    rhs = jnp.concatenate(
        [
            jnp.where(low, own, zero),
            jnp.where(low, partner, zero),
            jnp.where(low, zero, own),
            jnp.where(low, zero, partner),
        ],
        axis=0,
    )
    lhs = jnp.concatenate([f_low, f_high], axis=1)
    return jnp.dot(lhs, rhs, preferred_element_type=jnp.float32).astype(jnp.bfloat16)


def kernel(
    lo_levels,
    hi_levels,
    sources,
    leaf_in,
    local_mix,
    lo_mix,
    hi_mix,
    leaf_out,
    targets,
    src_v,
    in_v,
    loc_v,
    mix_v,
    out_v,
    tgt_v,
    work,
    own,
    recv,
    in_sem,
    loc_sem,
    mix_sem,
    out_sem,
    tgt_sem,
    send_sem,
    recv_sem,
):
    blocks, rank, leaf = leaf_in.shape
    vecs = sources.shape[0]
    half = blocks // 2
    local_levels = local_mix.shape[1]
    levels = lo_levels + hi_levels
    groups = half // GROUP
    hi, lo = lax.axis_index("hi"), lax.axis_index("lo")

    def flipped(index, bit):
        stride = 1 << bit
        return index + stride - 2 * stride * ((index // stride) % 2)

    partners = [(hi, flipped(lo, b)) for b in range(lo_levels)]
    partners += [(flipped(hi, b), lo) for b in range(hi_levels)]

    barrier = pltpu.get_barrier_semaphore()
    for partner in partners:
        pl.semaphore_signal(barrier, inc=1, device_id=partner, device_id_type=MESH)

    part = half // CHUNKS
    in_copies = []
    for c in range(CHUNKS):
        copies = []
        for side in range(2):
            first = side * half + c * part
            columns = pl.ds(first * leaf, part * leaf)
            rows = pl.ds(first, part)
            copies.append(
                pltpu.make_async_copy(
                    sources.at[:, columns], src_v.at[:, columns], in_sem.at[c, 2 * side]
                )
            )
            copies.append(
                pltpu.make_async_copy(leaf_in.at[rows], in_v.at[rows], in_sem.at[c, 2 * side + 1])
            )
        in_copies.append(copies)
    loc_copies = [
        pltpu.make_async_copy(local_mix.at[:, b], loc_v.at[b], loc_sem.at[b])
        for b in range(local_levels)
    ]
    mix_copies = [
        pltpu.make_async_copy(lo_mix.at[:, b], mix_v.at[b], mix_sem.at[b]) for b in range(lo_levels)
    ]
    mix_copies += [
        pltpu.make_async_copy(hi_mix.at[:, b], mix_v.at[lo_levels + b], mix_sem.at[lo_levels + b])
        for b in range(hi_levels)
    ]
    out_copy = pltpu.make_async_copy(leaf_out, out_v, out_sem.at[0])
    for copies in in_copies:
        for copy in copies:
            copy.start()
    for copy in loc_copies + mix_copies + [out_copy]:
        copy.start()

    for c in range(CHUNKS):
        for copy in in_copies[c]:
            copy.wait()

        def project(i, _):
            for u in range(UNROLL):
                j = c * part + i * UNROLL + u
                lhs = jnp.concatenate([in_v[j], in_v[j + half]], axis=0)
                low = pl.ds(pl.multiple_of(j * leaf, leaf), leaf)
                high = pl.ds(pl.multiple_of((j + half) * leaf, leaf), leaf)
                rhs = jnp.concatenate([src_v[:, low], src_v[:, high]], axis=0)
                both = lax.dot_general(
                    lhs, rhs, (((1,), (1,)), ((), ())), preferred_element_type=jnp.float32
                )
                tile = jnp.where(low_lanes((rank, 2 * vecs)), both[:rank], both[rank:])
                work[0, j] = tile.astype(jnp.bfloat16)
            return 0

        lax.fori_loop(0, part // UNROLL, project, 0)

    for b in range(local_levels - 1):
        loc_copies[b].wait()
        stride = 1 << b
        now, later = b % 2, (b + 1) % 2

        def pair(i, _):
            for u in range(UNROLL // 2):
                p = i * (UNROLL // 2) + u
                j = (p // stride) * (2 * stride) + p % stride
                k = j + stride
                first, second = work[now, j], work[now, k]
                work[later, j] = mixed(first, second, loc_v[b, j], loc_v[b, j + half])
                work[later, k] = mixed(second, first, loc_v[b, k], loc_v[b, k + half])
            return 0

        lax.fori_loop(0, half // UNROLL, pair, 0)
    final = (local_levels - 1) % 2
    loc_copies[local_levels - 1].wait()
    pl.semaphore_wait(barrier, levels)
    for copy in mix_copies + [out_copy]:
        copy.wait()

    def message(stage, g):
        tiles = pl.ds(g * GROUP, GROUP)
        return pltpu.make_async_remote_copy(
            own.at[stage, tiles],
            recv.at[stage, tiles],
            send_sem.at[stage],
            recv_sem.at[stage, g],
            device_id=partners[stage],
            device_id_type=MESH,
        )

    def run_stage(stage, g):
        if stage > 0:
            message(stage - 1, g).wait_recv()
        for u in range(GROUP):
            j = g * GROUP + u
            if stage == 0:
                tile = work[final, j]
                turned = jnp.concatenate([tile[:, vecs:], tile[:, :vecs]], axis=1)
                b = local_levels - 1
                own[0, j] = mixed(tile, turned, loc_v[b, j], loc_v[b, j + half])
            else:
                tile = mixed(
                    own[stage - 1, j],
                    recv[stage - 1, j],
                    mix_v[stage - 1, j],
                    mix_v[stage - 1, j + half],
                )
                if stage < levels:
                    own[stage, j] = tile
                else:
                    flat = tile.T
                    for side in range(2):
                        block = j + side * half
                        columns = pl.ds(pl.multiple_of(block * leaf, leaf), leaf)
                        result = jnp.dot(
                            flat[side * vecs : (side + 1) * vecs],
                            out_v[block],
                            preferred_element_type=jnp.float32,
                        )
                        tgt_v[:, columns] = result.astype(jnp.bfloat16)
        if stage < levels:
            message(stage, g).start()
        else:
            for side in range(2):
                start = (side * half + g * GROUP) * leaf
                columns = pl.ds(pl.multiple_of(start, leaf), GROUP * leaf)
                pltpu.make_async_copy(
                    tgt_v.at[:, columns], targets.at[:, columns], tgt_sem.at[0]
                ).start()

    def step(t, _):
        for stage in reversed(range(levels + 1)):
            g = t - OFFSETS[stage]

            @pl.when((g >= 0) & (g < groups))
            def _():
                run_stage(stage, g)

        return 0

    lax.fori_loop(0, groups + OFFSETS[levels], step, 0)

    for stage in range(levels):
        pltpu.make_async_remote_copy(
            own.at[stage],
            recv.at[stage],
            send_sem.at[stage],
            recv_sem.at[stage, 0],
            device_id=partners[stage],
            device_id_type=MESH,
        ).wait_send()
    pltpu.make_async_copy(tgt_v, targets, tgt_sem.at[0]).wait()


def body(sources, leaf_in, local_mix, lo_mix, hi_mix, leaf_out):
    blocks, rank, leaf = leaf_in.shape
    vecs = sources.shape[0]
    local_levels = local_mix.shape[1]
    lo_levels, hi_levels = lo_mix.shape[1], hi_mix.shape[1]
    levels = lo_levels + hi_levels
    half = blocks // 2
    tiles = (half, rank, 2 * vecs)
    dma = pltpu.SemaphoreType.DMA
    return pl.pallas_call(
        functools.partial(kernel, lo_levels, hi_levels),
        out_shape=jax.ShapeDtypeStruct(sources.shape, jnp.bfloat16),
        in_specs=[pl.BlockSpec(memory_space=pl.ANY)] * 6,
        out_specs=pl.BlockSpec(memory_space=pl.ANY),
        scratch_shapes=[
            pltpu.VMEM(sources.shape, jnp.bfloat16),
            pltpu.VMEM(leaf_in.shape, jnp.bfloat16),
            pltpu.VMEM((local_levels, blocks) + local_mix.shape[2:], jnp.bfloat16),
            pltpu.VMEM((levels, blocks) + local_mix.shape[2:], jnp.bfloat16),
            pltpu.VMEM(leaf_out.shape, jnp.bfloat16),
            pltpu.VMEM(sources.shape, jnp.bfloat16),
            pltpu.VMEM((2,) + tiles, jnp.bfloat16),
            pltpu.VMEM((levels,) + tiles, jnp.bfloat16),
            pltpu.VMEM((levels,) + tiles, jnp.bfloat16),
            dma((CHUNKS, 4)),
            dma((local_levels,)),
            dma((levels,)),
            dma((1,)),
            dma((1,)),
            dma((levels,)),
            dma((levels, half // GROUP)),
        ],
        compiler_params=pltpu.CompilerParams(
            collective_id=0, has_side_effects=True, vmem_limit_bytes=48 * 1024 * 1024
        ),
        name="butterfly",
    )(sources, leaf_in, local_mix, lo_mix, hi_mix, leaf_out)


def solution(mesh):
    return jax.shard_map(
        body,
        mesh=mesh,
        in_specs=(
            P(None, ("hi", "lo")),
            P(("hi", "lo"), None, None),
            P(("hi", "lo"), None, None, None),
            P(("hi", "lo"), None, None, None),
            P(("hi", "lo"), None, None, None),
            P(("hi", "lo"), None, None),
        ),
        out_specs=P(None, ("hi", "lo")),
        check_vma=False,
    )
```

time: 196 us -> 91.6 us (0.47)
  waiting for transfers between devices: 132 us -> 0 us
  Pallas kernels: 0 us -> 88.5 us
  matrix products: 30.5 us -> 0 us
  starting transfers between devices: 17 us -> 0 us
  local copies, waits for them, and re-layouts: 16 us -> 2.91 us
    ppermute x7 -> x0, waiting for transfers between devices: 132 us -> none  [swapped(): return lax.ppermute(block, axis, route)]
    pallas_call x0 -> x1, Pallas kernels: none -> 88.5 us  [body(): pl.pallas_call(functools.partial(kernel, lo_levels, hi_levels), out_shape...]
    dot_general x14 -> x0, matrix products: 30.5 us -> none  [the longest x12 23.3 us: mix_level(): jnp.einsum('kvs,kqs->kvq', joined, factors, preferred_element_type=jnp.fl...]
    ppermute x7 -> x0, starting transfers between devices: 17 us -> none  [swapped(): return lax.ppermute(block, axis, route)]
    rev x6 -> x0, local copies, waits for them, and re-layouts: 12.9 us -> none  [flip_blocks(): return lax.rev(grouped, (block_dim + 1,)).reshape(shape_now)]
    convert_element_type x1 -> x0, local copies, waits for them, and re-layouts: 3.04 us -> none  [body(): return result.reshape(vectors, blocks_here * leaf_size).astype(jnp.bfloat16)]
    unnamed x16 -> x3, local copies, waits for them, and re-layouts: 0.03 us -> 2.91 us
  transfers between devices with their start and end apart: 7 -> 0, of which waited for: 7 -> 0; matrix products, arithmetic and copies ran while one was open for 0% -> 0% of each run, Pallas kernels for 0% -> 0%
where the time goes in v1:
time: 91.6 us; the launch traced here: 91.4 us
  Pallas kernels  88.5 us (97%)
  local copies, waits for them, and re-layouts  2.91 us (3%)
    pallas_call x1, Pallas kernels, body(): pl.pallas_call(functools.partial(kernel, lo_levels, hi_levels), out_shape...  88.5 us
    unnamed x3, local copies, waits for them, and re-layouts  2.91 us

profile of v1, /device:TPU:0, one launch (start us, length us, event | category | flops | bytes accessed | tf_op | source)
XLA Modules:
  0.0 91.4 jit_solution(2500894067018166923)
XLA Ops:
  0.0 0.0 copy-start
  0.0 1.6 %copy-done = bf16[64,16384]{1,0:T(8,128)(2,1)S(1)} copy-done((bf16[64,16384]{1,0:T(8,128)(2,1)S(1)}, bf16[64,16384]{1,0:T(8,128)(2,1)}, u32[]{:S(2)}) %copy-start) | copy-done | bytes 2097176
  1.6 88.5 %butterfly.1 = bf16[64,16384]{1,0:T(8,128)(2,1)S(1)} custom-call(bf16[64,16384]{1,0:T(8,128)(2,1)S(1)} %copy-done, bf16[64,64,256]{2,1,0:T(8,128)(2,1)} %leaf_in.1, bf16[64,6,64,128]{3,2,1,0:T(8,128)(2,1)} %local_mix.1, bf16[64,3,64,128]{3,2,1,0:T(8,128)(2,1)} %lo_mix.1, bf16[64,4,64,128]{3,2,1,0:T(8,128)(2,1)} %hi_mix.1, bf16[64,64,256]{2,1,0:T(8,128)(2,1)} %leaf_out.1), custom_call_target="tpu_custom_call" | custom-call | tf_op jit(solution)/shard_map/butterfly/pallas_call | solution.py:244
  90.1 1.3 %copy.8 = bf16[64,16384]{1,0:T(8,128)(2,1)} copy(bf16[64,16384]{1,0:T(8,128)(2,1)S(1)} %butterfly.1) | data formatting | bytes 4194304
Async XLA Ops:
  0.0 1.6 %copy-start = (bf16[64,16384]{1,0:T(8,128)(2,1)S(1)}, bf16[64,16384]{1,0:T(8,128)(2,1)}, u32[]{:S(2)}) copy-start(bf16[64,16384]{1,0:T(8,128)(2,1)} %sources.1) | copy-start | bytes 6291460

commit v2 on v1

v2 whole, which is shorter than its diff:
```python
import functools

import jax
import jax.numpy as jnp
from jax import lax
from jax.experimental import pallas as pl
from jax.experimental.pallas import tpu as pltpu
from jax.sharding import PartitionSpec as P

MESH = pl.DeviceIdType.MESH
GROUP = 1
DELAYS = (2, 4, 5, 4, 5, 4, 5)
CHUNKS = 4
UNROLL = 16


def low_lanes(shape):
    return lax.broadcasted_iota(jnp.int32, shape, len(shape) - 1) < shape[-1] // 2


def mixed(own, partner, f_low, f_high):
    zero = jnp.zeros_like(own)
    low = low_lanes(own.shape)
    rhs = jnp.concatenate(
        [
            jnp.where(low, own, zero),
            jnp.where(low, partner, zero),
            jnp.where(low, zero, own),
            jnp.where(low, zero, partner),
        ],
        axis=0,
    )
    lhs = jnp.concatenate([f_low, f_high], axis=1)
    return jnp.dot(lhs, rhs, preferred_element_type=jnp.float32).astype(jnp.bfloat16)


def kernel(lo_levels, hi_levels, *refs):
    levels = lo_levels + hi_levels
    sources, leaf_in, local_mix, lo_mix, hi_mix, leaf_out, targets = refs[:7]
    src_v, in_v, loc_v, mix_v, out_v = refs[7:12]
    work = refs[12:14]
    own = refs[14 : 15 + levels]
    recv = refs[15 + levels : 15 + 2 * levels]
    in_sem, loc_sem, mix_sem, out_sem, send_sem, recv_sem = refs[15 + 2 * levels :]
    blocks, rank, leaf = leaf_in.shape
    vecs = sources.shape[0]
    half = blocks // 2
    local_levels = local_mix.shape[1]
    groups = half // GROUP
    hi, lo = lax.axis_index("hi"), lax.axis_index("lo")

    def flipped(index, bit):
        stride = 1 << bit
        return index + stride - 2 * stride * ((index // stride) % 2)

    partners = [(hi, flipped(lo, b)) for b in range(lo_levels)]
    partners += [(flipped(hi, b), lo) for b in range(hi_levels)]

    barrier = pltpu.get_barrier_semaphore()
    for partner in partners:
        pl.semaphore_signal(barrier, inc=1, device_id=partner, device_id_type=MESH)

    part = half // CHUNKS
    in_copies = []
    for c in range(CHUNKS):
        copies = []
        for side in range(2):
            first = side * half + c * part
            columns = pl.ds(first * leaf, part * leaf)
            rows = pl.ds(first, part)
            copies.append(
                pltpu.make_async_copy(
                    sources.at[:, columns], src_v.at[:, columns], in_sem.at[c, 2 * side]
                )
            )
            copies.append(
                pltpu.make_async_copy(leaf_in.at[rows], in_v.at[rows], in_sem.at[c, 2 * side + 1])
            )
        in_copies.append(copies)
    loc_copies = [
        pltpu.make_async_copy(local_mix.at[:, b], loc_v.at[b], loc_sem.at[b])
        for b in range(local_levels)
    ]
    held = pl.ds(GROUP, half)
    mix_copies, out_copies = [], []
    for b in range(levels):
        mix = lo_mix.at[:, b] if b < lo_levels else hi_mix.at[:, b - lo_levels]
        mix_copies.append(
            [
                pltpu.make_async_copy(
                    mix.at[pl.ds(side * half, half)], mix_v.at[b, side, held], mix_sem.at[b, side]
                )
                for side in range(2)
            ]
        )
    for side in range(2):
        out_copies.append(
            pltpu.make_async_copy(
                leaf_out.at[pl.ds(side * half, half)], out_v.at[side, held], out_sem.at[side]
            )
        )
    for copies in in_copies + [loc_copies] + mix_copies + [out_copies]:
        for copy in copies:
            copy.start()

    for c in range(CHUNKS):
        for copy in in_copies[c]:
            copy.wait()
        for j in range(c * part, (c + 1) * part):
            lhs = jnp.concatenate([in_v[j], in_v[j + half]], axis=0)
            low, high = pl.ds(j * leaf, leaf), pl.ds((j + half) * leaf, leaf)
            rhs = jnp.concatenate([src_v[:, low], src_v[:, high]], axis=0)
            both = lax.dot_general(
                lhs, rhs, (((1,), (1,)), ((), ())), preferred_element_type=jnp.float32
            )
            tile = jnp.where(low_lanes((rank, 2 * vecs)), both[:rank], both[rank:])
            work[0][j] = tile.astype(jnp.bfloat16)

    for b in range(local_levels - 1):
        loc_copies[b].wait()
        stride = 1 << b
        now, later = work[b % 2], work[(b + 1) % 2]

        def pair(i, _):
            for u in range(UNROLL // 2):
                p = i * (UNROLL // 2) + u
                j = (p // stride) * (2 * stride) + p % stride
                k = j + stride
                first, second = now[j], now[k]
                later[j] = mixed(first, second, loc_v[b, j], loc_v[b, j + half])
                later[k] = mixed(second, first, loc_v[b, k], loc_v[b, k + half])
            return 0

        lax.fori_loop(0, half // UNROLL, pair, 0)
    last = local_levels - 1
    entered = work[last % 2]
    loc_copies[last].wait()
    pl.semaphore_wait(barrier, levels)

    starts = [0]
    for delay in DELAYS[:levels]:
        starts.append(starts[-1] + delay)
    starts.append(starts[-1] + 1)

    def message(stage, g):
        tiles = pl.ds((g + 1) * GROUP, GROUP)
        return pltpu.make_async_remote_copy(
            own[stage].at[tiles],
            recv[stage].at[tiles],
            send_sem.at[stage],
            recv_sem.at[stage, g],
            device_id=partners[stage],
            device_id_type=MESH,
        )

    def step(t, _):
        for stage in range(levels + 1):
            g = t - starts[stage]
            if stage > 0:

                @pl.when((g >= 0) & (g < groups))
                def _():
                    message(stage - 1, g).wait_recv()

                @pl.when(g == 0)
                def _():
                    for copy in mix_copies[stage - 1]:
                        copy.wait()

        @pl.when(t == starts[levels + 1])
        def _():
            for copy in out_copies:
                copy.wait()

        for u in range(GROUP):
            g = t - starts[levels + 1]
            place = (jnp.maximum(g, -1) + 1) * GROUP + u
            j = jnp.maximum(g, 0) * GROUP + u
            flat = own[levels][place].T
            for side in range(2):
                block = j + side * half
                columns = pl.ds(pl.multiple_of(block * leaf, leaf), leaf)
                result = jnp.dot(
                    flat[side * vecs : (side + 1) * vecs],
                    out_v[side, place],
                    preferred_element_type=jnp.float32,
                )
                targets[:, columns] = result.astype(jnp.bfloat16)
            for stage in reversed(range(levels + 1)):
                g = t - starts[stage]
                place = (jnp.minimum(jnp.maximum(g, -1), groups) + 1) * GROUP + u
                known = jnp.minimum(place, half + u)
                j = jnp.minimum(jnp.maximum(g, 0), groups - 1) * GROUP + u
                if stage > 0:
                    own[stage][place] = mixed(
                        own[stage - 1][place],
                        recv[stage - 1][place],
                        mix_v[stage - 1, 0, known],
                        mix_v[stage - 1, 1, known],
                    )
                else:
                    tile = entered[j]
                    turned = jnp.concatenate([tile[:, vecs:], tile[:, :vecs]], axis=1)
                    own[0][place] = mixed(tile, turned, loc_v[last, j], loc_v[last, j + half])

        for stage in range(levels):
            g = t - starts[stage]

            @pl.when((g >= 0) & (g < groups))
            def _():
                message(stage, g).start()

        return 0

    lax.fori_loop(0, groups + starts[levels + 1], step, 0)

    for stage in range(levels):
        pltpu.make_async_remote_copy(
            own[stage].at[held],
            recv[stage].at[held],
            send_sem.at[stage],
            recv_sem.at[stage, 0],
            device_id=partners[stage],
            device_id_type=MESH,
        ).wait_send()


def body(sources, leaf_in, local_mix, lo_mix, hi_mix, leaf_out):
    blocks, rank, _ = leaf_in.shape
    vecs = sources.shape[0]
    local_levels = local_mix.shape[1]
    lo_levels, hi_levels = lo_mix.shape[1], hi_mix.shape[1]
    levels = lo_levels + hi_levels
    half = blocks // 2
    factors = (blocks,) + local_mix.shape[2:]
    bf16, dma = jnp.bfloat16, pltpu.SemaphoreType.DMA
    spared = pltpu.VMEM((half + 2 * GROUP, rank, 2 * vecs), bf16)
    return pl.pallas_call(
        functools.partial(kernel, lo_levels, hi_levels),
        out_shape=jax.ShapeDtypeStruct(sources.shape, bf16),
        in_specs=[pl.BlockSpec(memory_space=pltpu.HBM)] * 6,
        out_specs=pl.BlockSpec(memory_space=pltpu.VMEM),
        scratch_shapes=[
            pltpu.VMEM(sources.shape, bf16),
            pltpu.VMEM(leaf_in.shape, bf16),
            pltpu.VMEM((local_levels,) + factors, bf16),
            pltpu.VMEM((levels, 2, half + GROUP) + factors[1:], bf16),
            pltpu.VMEM((2, half + GROUP) + leaf_out.shape[1:], bf16),
        ]
        + [pltpu.VMEM((half, rank, 2 * vecs), bf16)] * 2
        + [spared] * (2 * levels + 1)
        + [
            dma((CHUNKS, 4)),
            dma((local_levels,)),
            dma((levels, 2)),
            dma((2,)),
            dma((levels,)),
            dma((levels, half // GROUP)),
        ],
        compiler_params=pltpu.CompilerParams(
            collective_id=0, has_side_effects=True, vmem_limit_bytes=50 * 1024 * 1024
        ),
        name="butterfly",
    )(sources, leaf_in, local_mix, lo_mix, hi_mix, leaf_out)


def solution(mesh):
    return jax.shard_map(
        body,
        mesh=mesh,
        in_specs=(
            P(None, ("hi", "lo")),
            P(("hi", "lo"), None, None),
            P(("hi", "lo"), None, None, None),
            P(("hi", "lo"), None, None, None),
            P(("hi", "lo"), None, None, None),
            P(("hi", "lo"), None, None),
        ),
        out_specs=P(None, ("hi", "lo")),
        check_vma=False,
    )
```

time: 91.6 us -> 67 us (0.73)
  Pallas kernels: 88.5 us -> 65.6 us
  local copies, waits for them, and re-layouts: 2.91 us -> 1.32 us
    pallas_call x1, Pallas kernels: 88.5 us -> 65.6 us  [body(): pl.pallas_call(functools.partial(kernel, lo_levels, hi_levels), out_shape...]
    unnamed x3 -> x1, local copies, waits for them, and re-layouts: 2.91 us -> 1.32 us
where the time goes in v2:
time: 67 us; the launch traced here: 66.9 us
  Pallas kernels  65.6 us (98%)
  local copies, waits for them, and re-layouts  1.32 us (2%)
    pallas_call x1, Pallas kernels, body(): pl.pallas_call(functools.partial(kernel, lo_levels, hi_levels), out_shape...  65.6 us

profile of v2, /device:TPU:0, one launch (start us, length us, event | category | flops | bytes accessed | tf_op | source)
XLA Modules:
  0.0 66.9 jit_solution(1656958590952271504)
XLA Ops:
  0.0 65.6 %butterfly.1 = bf16[64,16384]{1,0:T(8,128)(2,1)S(1)} custom-call(bf16[64,16384]{1,0:T(8,128)(2,1)} %refs_0_.1, bf16[64,64,256]{2,1,0:T(8,128)(2,1)} %refs_1_.1, bf16[64,6,64,128]{3,2,1,0:T(8,128)(2,1)} %refs_2_.1, bf16[64,3,64,128]{3,2,1,0:T(8,128)(2,1)} %refs_3_.1, bf16[64,4,64,128]{3,2,1,0:T(8,128)(2,1)} %refs_4_.1, bf16[64,64,256]{2,1,0:T(8,128)(2,1)} %refs_5_.1), custom_call_target="tpu_custom_call" | custom-call | tf_op jit(solution)/shard_map/butterfly/pallas_call | solution.py:238
  65.6 1.3 %copy.8 = bf16[64,16384]{1,0:T(8,128)(2,1)} copy(bf16[64,16384]{1,0:T(8,128)(2,1)S(1)} %butterfly.1) | data formatting | bytes 4194304

commit v3 on v2

--- a/solution.py
+++ b/solution.py
@@ -8,10 +8,14 @@
 from jax.sharding import PartitionSpec as P
 
 MESH = pl.DeviceIdType.MESH
+EARLY = 1
+LOCAT = 1
+LATE = 1
 GROUP = 1
-DELAYS = (2, 4, 5, 4, 5, 4, 5)
+DELAYS = (2, 5, 6, 5, 6, 5, 6)
 CHUNKS = 4
-UNROLL = 16
+BLOCKS = ((8, 7, 6, 5), (4, 3, 2, 1, 0))
+UNROLL = 32
 
 
 def low_lanes(shape):
@@ -99,13 +103,18 @@
                 leaf_out.at[pl.ds(side * half, half)], out_v.at[side, held], out_sem.at[side]
             )
         )
-    for copies in in_copies + [loc_copies] + mix_copies + [out_copies]:
-        for copy in copies:
-            copy.start()
+    def begin(batches):
+        for copies in batches:
+            for copy in copies:
+                copy.start()
+
+    begin(in_copies + [loc_copies[:EARLY]])
 
     for c in range(CHUNKS):
         for copy in in_copies[c]:
             copy.wait()
+        if c == LOCAT:
+            begin([loc_copies[EARLY:]])
         for j in range(c * part, (c + 1) * part):
             lhs = jnp.concatenate([in_v[j], in_v[j + half]], axis=0)
             low, high = pl.ds(j * leaf, leaf), pl.ds((j + half) * leaf, leaf)
@@ -132,6 +141,8 @@
             return 0
 
         lax.fori_loop(0, half // UNROLL, pair, 0)
+        if b == LATE:
+            begin(mix_copies + [out_copies])
     last = local_levels - 1
     entered = work[last % 2]
     loc_copies[last].wait()
@@ -153,62 +164,73 @@
             device_id_type=MESH,
         )
 
+    def receive(stage, g):
+        @pl.when((g >= 0) & (g < groups))
+        def _():
+            message(stage - 1, g).wait_recv()
+
+        @pl.when(g == 0)
+        def _():
+            for copy in mix_copies[stage - 1]:
+                copy.wait()
+
+    def mix(stage, g, u):
+        place = (jnp.minimum(jnp.maximum(g, -1), groups) + 1) * GROUP + u
+        if stage > 0:
+            known = jnp.minimum(place, half + u)
+            own[stage][place] = mixed(
+                own[stage - 1][place],
+                recv[stage - 1][place],
+                mix_v[stage - 1, 0, known],
+                mix_v[stage - 1, 1, known],
+            )
+        else:
+            j = jnp.minimum(jnp.maximum(g, 0), groups - 1) * GROUP + u
+            tile = entered[j]
+            turned = jnp.concatenate([tile[:, vecs:], tile[:, :vecs]], axis=1)
+            own[0][place] = mixed(tile, turned, loc_v[last, j], loc_v[last, j + half])
+
+    def interpolate(g, u):
+        place = (jnp.maximum(g, -1) + 1) * GROUP + u
+        j = jnp.maximum(g, 0) * GROUP + u
+        flat = own[levels][place].T
+        for side in range(2):
+            columns = pl.ds(pl.multiple_of((j + side * half) * leaf, leaf), leaf)
+            result = jnp.dot(
+                flat[side * vecs : (side + 1) * vecs],
+                out_v[side, place],
+                preferred_element_type=jnp.float32,
+            )
+            targets[:, columns] = result.astype(jnp.bfloat16)
+
     def step(t, _):
-        for stage in range(levels + 1):
-            g = t - starts[stage]
-            if stage > 0:
-
-                @pl.when((g >= 0) & (g < groups))
+        for block in BLOCKS:
+            for stage in block:
+                if 0 < stage <= levels:
+                    receive(stage, t - starts[stage])
+            if levels + 1 in block:
+
+                @pl.when(t == starts[levels + 1])
                 def _():
-                    message(stage - 1, g).wait_recv()
-
-                @pl.when(g == 0)
-                def _():
-                    for copy in mix_copies[stage - 1]:
+                    for copy in out_copies:
                         copy.wait()
 
-        @pl.when(t == starts[levels + 1])
-        def _():
-            for copy in out_copies:
-                copy.wait()
-
-        for u in range(GROUP):
-            g = t - starts[levels + 1]
-            place = (jnp.maximum(g, -1) + 1) * GROUP + u
-            j = jnp.maximum(g, 0) * GROUP + u
-            flat = own[levels][place].T
-            for side in range(2):
-                block = j + side * half
-                columns = pl.ds(pl.multiple_of(block * leaf, leaf), leaf)
-                result = jnp.dot(
-                    flat[side * vecs : (side + 1) * vecs],
-                    out_v[side, place],
-                    preferred_element_type=jnp.float32,
-                )
-                targets[:, columns] = result.astype(jnp.bfloat16)
-            for stage in reversed(range(levels + 1)):
+            @pl.when((t >= starts[min(block)]) & (t < starts[max(block)] + groups))
+            def _():
+                for u in range(GROUP):
+                    for stage in block:
+                        if stage > levels:
+                            interpolate(t - starts[stage], u)
+                        else:
+                            mix(stage, t - starts[stage], u)
+
+            for stage in block:
                 g = t - starts[stage]
-                place = (jnp.minimum(jnp.maximum(g, -1), groups) + 1) * GROUP + u
-                known = jnp.minimum(place, half + u)
-                j = jnp.minimum(jnp.maximum(g, 0), groups - 1) * GROUP + u
-                if stage > 0:
-                    own[stage][place] = mixed(
-                        own[stage - 1][place],
-                        recv[stage - 1][place],
-                        mix_v[stage - 1, 0, known],
-                        mix_v[stage - 1, 1, known],
-                    )
-                else:
-                    tile = entered[j]
-                    turned = jnp.concatenate([tile[:, vecs:], tile[:, :vecs]], axis=1)
-                    own[0][place] = mixed(tile, turned, loc_v[last, j], loc_v[last, j + half])
-
-        for stage in range(levels):
-            g = t - starts[stage]
-
-            @pl.when((g >= 0) & (g < groups))
-            def _():
-                message(stage, g).start()
+                if stage < levels:
+
+                    @pl.when((g >= 0) & (g < groups))
+                    def _():
+                        message(stage, g).start()
 
         return 0
 

time: 67 us -> 59.1 us (0.88)
  Pallas kernels: 65.6 us -> 57.7 us
    pallas_call x1, Pallas kernels: 65.6 us -> 57.7 us  [body(): pl.pallas_call(functools.partial(kernel, lo_levels, hi_levels), out_shape...]
where the time goes in v3:
time: 59.1 us; the launch traced here: 59 us
  Pallas kernels  57.7 us (98%)
  local copies, waits for them, and re-layouts  1.32 us (2%)
    pallas_call x1, Pallas kernels, body(): pl.pallas_call(functools.partial(kernel, lo_levels, hi_levels), out_shape...  57.7 us
    unnamed x1, local copies, waits for them, and re-layouts  1.32 us

profile of v3, /device:TPU:0, one launch (start us, length us, event | category | flops | bytes accessed | tf_op | source)
XLA Modules:
  0.0 59.0 jit_solution(2721134834622368369)
XLA Ops:
  0.0 57.7 %butterfly.1 = bf16[64,16384]{1,0:T(8,128)(2,1)S(1)} custom-call(bf16[64,16384]{1,0:T(8,128)(2,1)} %refs_0_.1, bf16[64,64,256]{2,1,0:T(8,128)(2,1)} %refs_1_.1, bf16[64,6,64,128]{3,2,1,0:T(8,128)(2,1)} %refs_2_.1, bf16[64,3,64,128]{3,2,1,0:T(8,128)(2,1)} %refs_3_.1, bf16[64,4,64,128]{3,2,1,0:T(8,128)(2,1)} %refs_4_.1, bf16[64,64,256]{2,1,0:T(8,128)(2,1)} %refs_5_.1), custom_call_target="tpu_custom_call" | custom-call | tf_op jit(solution)/shard_map/butterfly/pallas_call | solution.py:260
  57.7 1.3 %copy.8 = bf16[64,16384]{1,0:T(8,128)(2,1)} copy(bf16[64,16384]{1,0:T(8,128)(2,1)S(1)} %butterfly.1) | data formatting | bytes 4194304

commit v4 on v3

--- a/solution.py
+++ b/solution.py
@@ -8,11 +8,9 @@
 from jax.sharding import PartitionSpec as P
 
 MESH = pl.DeviceIdType.MESH
-EARLY = 1
-LOCAT = 1
 LATE = 1
 GROUP = 1
-DELAYS = (2, 5, 6, 5, 6, 5, 6)
+DELAYS = (3, 5, 6, 5, 6, 5, 6)
 CHUNKS = 4
 BLOCKS = ((8, 7, 6, 5), (4, 3, 2, 1, 0))
 UNROLL = 32
@@ -103,18 +101,15 @@
                 leaf_out.at[pl.ds(side * half, half)], out_v.at[side, held], out_sem.at[side]
             )
         )
-    def begin(batches):
-        for copies in batches:
-            for copy in copies:
-                copy.start()
-
-    begin(in_copies + [loc_copies[:EARLY]])
+    for copies in in_copies:
+        for copy in copies:
+            copy.start(priority=0)
+    for copy in loc_copies:
+        copy.start(priority=1)
 
     for c in range(CHUNKS):
         for copy in in_copies[c]:
             copy.wait()
-        if c == LOCAT:
-            begin([loc_copies[EARLY:]])
         for j in range(c * part, (c + 1) * part):
             lhs = jnp.concatenate([in_v[j], in_v[j + half]], axis=0)
             low, high = pl.ds(j * leaf, leaf), pl.ds((j + half) * leaf, leaf)
@@ -127,6 +122,10 @@
 
     for b in range(local_levels - 1):
         loc_copies[b].wait()
+        if b == LATE:
+            for copies in mix_copies + [out_copies]:
+                for copy in copies:
+                    copy.start(priority=1)
         stride = 1 << b
         now, later = work[b % 2], work[(b + 1) % 2]
 
@@ -141,8 +140,6 @@
             return 0
 
         lax.fori_loop(0, half // UNROLL, pair, 0)
-        if b == LATE:
-            begin(mix_copies + [out_copies])
     last = local_levels - 1
     entered = work[last % 2]
     loc_copies[last].wait()

time: 59.1 us -> 59.1 us (level)
  no operation moved by 1% of the time
where the time goes in v4:
time: 59.1 us; the launch traced here: 59 us
  Pallas kernels  57.7 us (98%)
  local copies, waits for them, and re-layouts  1.32 us (2%)
    pallas_call x1, Pallas kernels, body(): pl.pallas_call(functools.partial(kernel, lo_levels, hi_levels), out_shape...  57.7 us
    unnamed x1, local copies, waits for them, and re-layouts  1.32 us

profile of v4, /device:TPU:0, one launch (start us, length us, event | category | flops | bytes accessed | tf_op | source)
XLA Modules:
  0.0 59.0 jit_solution(16129874563765704285)
XLA Ops:
  0.0 57.7 %butterfly.1 = bf16[64,16384]{1,0:T(8,128)(2,1)S(1)} custom-call(bf16[64,16384]{1,0:T(8,128)(2,1)} %refs_0_.1, bf16[64,64,256]{2,1,0:T(8,128)(2,1)} %refs_1_.1, bf16[64,6,64,128]{3,2,1,0:T(8,128)(2,1)} %refs_2_.1, bf16[64,3,64,128]{3,2,1,0:T(8,128)(2,1)} %refs_3_.1, bf16[64,4,64,128]{3,2,1,0:T(8,128)(2,1)} %refs_4_.1, bf16[64,64,256]{2,1,0:T(8,128)(2,1)} %refs_5_.1), custom_call_target="tpu_custom_call" | custom-call | tf_op jit(solution)/shard_map/butterfly/pallas_call | solution.py:257
  57.7 1.3 %copy.8 = bf16[64,16384]{1,0:T(8,128)(2,1)} copy(bf16[64,16384]{1,0:T(8,128)(2,1)S(1)} %butterfly.1) | data formatting | bytes 4194304

commit v5 on v4

--- a/solution.py
+++ b/solution.py
@@ -9,10 +9,13 @@
 
 MESH = pl.DeviceIdType.MESH
 LATE = 1
+TWO = 24
+FARN = 8
+DIRECT = 7
 GROUP = 1
 DELAYS = (3, 5, 6, 5, 6, 5, 6)
 CHUNKS = 4
-BLOCKS = ((8, 7, 6, 5), (4, 3, 2, 1, 0))
+BLOCKS = ((10, 9), (8, 7, 6, 5), (4, 3, 2, 1, 0))
 UNROLL = 32
 
 
@@ -42,13 +45,15 @@
     src_v, in_v, loc_v, mix_v, out_v = refs[7:12]
     work = refs[12:14]
     own = refs[14 : 15 + levels]
-    recv = refs[15 + levels : 15 + 2 * levels]
-    in_sem, loc_sem, mix_sem, out_sem, send_sem, recv_sem = refs[15 + 2 * levels :]
+    recv = refs[15 + levels : 16 + 2 * levels]
+    far_v = refs[16 + 2 * levels]
+    in_sem, loc_sem, mix_sem, out_sem, send_sem, recv_sem, far_send, far_recv = refs[17 + 2 * levels :]
     blocks, rank, leaf = leaf_in.shape
     vecs = sources.shape[0]
     half = blocks // 2
     local_levels = local_mix.shape[1]
     groups = half // GROUP
+    far_tiles = (groups - TWO) * GROUP // (FARN // 2)
     hi, lo = lax.axis_index("hi"), lax.axis_index("lo")
 
     def flipped(index, bit):
@@ -57,6 +62,7 @@
 
     partners = [(hi, flipped(lo, b)) for b in range(lo_levels)]
     partners += [(flipped(hi, b), lo) for b in range(hi_levels)]
+    partners.append((flipped(flipped(hi, hi_levels - 2), hi_levels - 1), lo))
 
     barrier = pltpu.get_barrier_semaphore()
     for partner in partners:
@@ -107,9 +113,24 @@
     for copy in loc_copies:
         copy.start(priority=1)
 
+    def far(k):
+        side, first = k % 2, TWO * GROUP + k // 2 * far_tiles
+        return pltpu.make_async_remote_copy(
+            hi_mix.at[pl.ds(side * half + first, far_tiles), hi_levels - 2],
+            far_v.at[side, pl.ds(GROUP + first, far_tiles)],
+            far_send.at[k],
+            far_recv.at[k],
+            device_id=partners[levels - 1],
+            device_id_type=MESH,
+        )
+
     for c in range(CHUNKS):
         for copy in in_copies[c]:
             copy.wait()
+        if c == 0:
+            pl.semaphore_wait(barrier, levels + 1)
+            for k in range(FARN):
+                far(k).start()
         for j in range(c * part, (c + 1) * part):
             lhs = jnp.concatenate([in_v[j], in_v[j + half]], axis=0)
             low, high = pl.ds(j * leaf, leaf), pl.ds((j + half) * leaf, leaf)
@@ -143,53 +164,88 @@
     last = local_levels - 1
     entered = work[last % 2]
     loc_copies[last].wait()
-    pl.semaphore_wait(barrier, levels)
-
+
+    near, both = levels - 2, levels + 2
     starts = [0]
-    for delay in DELAYS[:levels]:
+    for delay in DELAYS:
         starts.append(starts[-1] + delay)
     starts.append(starts[-1] + 1)
-
-    def message(stage, g):
+    starts += [starts[near] + DIRECT, starts[near] + DIRECT + 1]
+    spans = [(0, groups)] * (near + 1) + [(0, TWO)] * 3 + [(TWO, groups)] * 2
+
+    def message(level, g, source):
         tiles = pl.ds((g + 1) * GROUP, GROUP)
         return pltpu.make_async_remote_copy(
-            own[stage].at[tiles],
-            recv[stage].at[tiles],
-            send_sem.at[stage],
-            recv_sem.at[stage, g],
-            device_id=partners[stage],
+            own[source].at[tiles],
+            recv[level].at[tiles],
+            send_sem.at[level],
+            recv_sem.at[level, g],
+            device_id=partners[level],
             device_id_type=MESH,
         )
 
     def receive(stage, g):
-        @pl.when((g >= 0) & (g < groups))
+        first, end = spans[stage]
+        wanted = (near, near + 1, near + 2) if stage == both else (stage - 1,)
+
+        @pl.when((g >= first) & (g < end))
         def _():
-            message(stage - 1, g).wait_recv()
-
-        @pl.when(g == 0)
-        def _():
-            for copy in mix_copies[stage - 1]:
-                copy.wait()
+            for level in wanted:
+                message(level, g, 0).wait_recv()
+
+        if stage == both:
+            count = far_tiles // GROUP
+
+            @pl.when((g >= first) & (g < end) & ((g - first) % count == 0))
+            def _():
+                for side in range(2):
+                    k = (g - first) // count * 2 + side
+                    rows = pl.ds((g + 1) * GROUP, far_tiles)
+                    pltpu.make_async_remote_copy(
+                        far_v.at[side, rows],
+                        far_v.at[side, rows],
+                        far_send.at[k],
+                        far_recv.at[k],
+                        device_id=partners[levels - 1],
+                        device_id_type=MESH,
+                    ).wait_recv()
+
+        else:
+
+            @pl.when(g == 0)
+            def _():
+                for copy in mix_copies[stage - 1]:
+                    copy.wait()
+
+    def located(stage, g, u):
+        first, end = spans[stage]
+        inside = jnp.clip(g - first + 1, 0, 1) * jnp.clip(end - g, 0, 1)
+        return inside * (g + 1) * GROUP + u
+
+    def factors(level, place):
+        return mix_v[level, 0, place], mix_v[level, 1, place]
 
     def mix(stage, g, u):
-        place = (jnp.minimum(jnp.maximum(g, -1), groups) + 1) * GROUP + u
-        if stage > 0:
-            known = jnp.minimum(place, half + u)
+        place = located(stage, g, u)
+        if stage == both:
+            a, b = near, near + 1
+            here = mixed(own[a][place], recv[a][place], *factors(a, place))
+            there = mixed(recv[b][place], recv[b + 1][place], far_v[0, place], far_v[1, place])
+            own[levels][place] = mixed(here, there, *factors(b, place))
+        elif stage > 0:
             own[stage][place] = mixed(
-                own[stage - 1][place],
-                recv[stage - 1][place],
-                mix_v[stage - 1, 0, known],
-                mix_v[stage - 1, 1, known],
+                own[stage - 1][place], recv[stage - 1][place], *factors(stage - 1, place)
             )
         else:
-            j = jnp.minimum(jnp.maximum(g, 0), groups - 1) * GROUP + u
+            j = jnp.clip(g, 0, groups - 1) * GROUP + u
             tile = entered[j]
             turned = jnp.concatenate([tile[:, vecs:], tile[:, :vecs]], axis=1)
             own[0][place] = mixed(tile, turned, loc_v[last, j], loc_v[last, j + half])
 
-    def interpolate(g, u):
-        place = (jnp.maximum(g, -1) + 1) * GROUP + u
-        j = jnp.maximum(g, 0) * GROUP + u
+    def interpolate(stage, g, u):
+        first, end = spans[stage]
+        place = located(stage, g, u)
+        j = jnp.clip(g, first, end - 1) * GROUP + u
         flat = own[levels][place].T
         for side in range(2):
             columns = pl.ds(pl.multiple_of((j + side * half) * leaf, leaf), leaf)
@@ -203,7 +259,7 @@
     def step(t, _):
         for block in BLOCKS:
             for stage in block:
-                if 0 < stage <= levels:
+                if stage not in (0, levels + 1, levels + 3):
                     receive(stage, t - starts[stage])
             if levels + 1 in block:
 
@@ -212,34 +268,50 @@
                     for copy in out_copies:
                         copy.wait()
 
-            @pl.when((t >= starts[min(block)]) & (t < starts[max(block)] + groups))
+            enter = min(starts[s] + spans[s][0] for s in block)
+            leave = max(starts[s] + spans[s][1] for s in block)
+
+            @pl.when((t >= enter) & (t < leave))
             def _():
                 for u in range(GROUP):
                     for stage in block:
-                        if stage > levels:
-                            interpolate(t - starts[stage], u)
+                        if stage in (levels + 1, levels + 3):
+                            interpolate(stage, t - starts[stage], u)
                         else:
                             mix(stage, t - starts[stage], u)
 
             for stage in block:
                 g = t - starts[stage]
+                first, end = spans[stage]
                 if stage < levels:
 
-                    @pl.when((g >= 0) & (g < groups))
+                    @pl.when((g >= first) & (g < end))
                     def _():
-                        message(stage, g).start()
+                        message(stage, g, stage).start()
+
+                if stage == near:
+
+                    @pl.when((g >= TWO) & (g < groups))
+                    def _():
+                        message(near + 1, g, near).start()
+                        message(near + 2, g, near).start()
 
         return 0
 
-    lax.fori_loop(0, groups + starts[levels + 1], step, 0)
-
-    for stage in range(levels):
+    steps = max(starts[s] + spans[s][1] for s in (levels + 1, levels + 3))
+    lax.fori_loop(0, steps, step, 0)
+
+    for k in range(FARN):
+        far(k).wait_send()
+    for level in range(levels + 1):
+        first = TWO if level == levels else 0
+        tiles = pl.ds((first + 1) * GROUP, (groups - first) * GROUP)
         pltpu.make_async_remote_copy(
-            own[stage].at[held],
-            recv[stage].at[held],
-            send_sem.at[stage],
-            recv_sem.at[stage, 0],
-            device_id=partners[stage],
+            own[0].at[tiles],
+            recv[level].at[tiles],
+            send_sem.at[level],
+            recv_sem.at[level, 0],
+            device_id=partners[level],
             device_id_type=MESH,
         ).wait_send()
 
@@ -267,17 +339,20 @@
             pltpu.VMEM((2, half + GROUP) + leaf_out.shape[1:], bf16),
         ]
         + [pltpu.VMEM((half, rank, 2 * vecs), bf16)] * 2
-        + [spared] * (2 * levels + 1)
+        + [spared] * (2 * levels + 2)
+        + [pltpu.VMEM((2, half + GROUP) + factors[1:], bf16)]
         + [
             dma((CHUNKS, 4)),
             dma((local_levels,)),
             dma((levels, 2)),
             dma((2,)),
-            dma((levels,)),
-            dma((levels, half // GROUP)),
+            dma((levels + 1,)),
+            dma((levels + 1, half // GROUP)),
+            dma((FARN,)),
+            dma((FARN,)),
         ],
         compiler_params=pltpu.CompilerParams(
-            collective_id=0, has_side_effects=True, vmem_limit_bytes=50 * 1024 * 1024
+            collective_id=0, has_side_effects=True, vmem_limit_bytes=51 * 1024 * 1024
         ),
         name="butterfly",
     )(sources, leaf_in, local_mix, lo_mix, hi_mix, leaf_out)

time: 59.1 us -> 58.3 us (0.986)
  Pallas kernels: 57.7 us -> 56.9 us
    pallas_call x1, Pallas kernels: 57.7 us -> 56.9 us  [body(): pl.pallas_call(functools.partial(kernel, lo_levels, hi_levels), out_shape...]
where the time goes in v5:
time: 58.3 us; the launch traced here: 58.2 us
  Pallas kernels  56.9 us (98%)
  local copies, waits for them, and re-layouts  1.32 us (2%)
    pallas_call x1, Pallas kernels, body(): pl.pallas_call(functools.partial(kernel, lo_levels, hi_levels), out_shape...  56.9 us
    unnamed x1, local copies, waits for them, and re-layouts  1.32 us

profile of v5, /device:TPU:0, one launch (start us, length us, event | category | flops | bytes accessed | tf_op | source)
XLA Modules:
  0.0 58.2 jit_solution(9228801775140164570)
XLA Ops:
  0.0 56.9 %butterfly.1 = bf16[64,16384]{1,0:T(8,128)(2,1)S(1)} custom-call(bf16[64,16384]{1,0:T(8,128)(2,1)} %refs_0_.1, bf16[64,64,256]{2,1,0:T(8,128)(2,1)} %refs_1_.1, bf16[64,6,64,128]{3,2,1,0:T(8,128)(2,1)} %refs_2_.1, bf16[64,3,64,128]{3,2,1,0:T(8,128)(2,1)} %refs_3_.1, bf16[64,4,64,128]{3,2,1,0:T(8,128)(2,1)} %refs_4_.1, bf16[64,64,256]{2,1,0:T(8,128)(2,1)} %refs_5_.1), custom_call_target="tpu_custom_call" | custom-call | tf_op jit(solution)/shard_map/butterfly/pallas_call | solution.py:329
  56.9 1.3 %copy.8 = bf16[64,16384]{1,0:T(8,128)(2,1)} copy(bf16[64,16384]{1,0:T(8,128)(2,1)S(1)} %butterfly.1) | data formatting | bytes 4194304

commit v6 on v5

--- a/solution.py
+++ b/solution.py
@@ -13,7 +13,7 @@
 FARN = 8
 DIRECT = 7
 GROUP = 1
-DELAYS = (3, 5, 6, 5, 6, 5, 6)
+DELAYS = (4, 5, 6, 5, 6, 5, 6)
 CHUNKS = 4
 BLOCKS = ((10, 9), (8, 7, 6, 5), (4, 3, 2, 1, 0))
 UNROLL = 32

time: 58.3 us -> 58.5 us (level)
  no operation moved by 1% of the time
where the time goes in v6:
time: 58.5 us; the launch traced here: 58.4 us
  Pallas kernels  57 us (97%)
  local copies, waits for them, and re-layouts  1.32 us (2%)
    pallas_call x1, Pallas kernels, body(): pl.pallas_call(functools.partial(kernel, lo_levels, hi_levels), out_shape...  57 us
    unnamed x1, local copies, waits for them, and re-layouts  1.32 us

profile of v6, /device:TPU:0, one launch (start us, length us, event | category | flops | bytes accessed | tf_op | source)
XLA Modules:
  0.0 58.4 jit_solution(16864463708882936781)
XLA Ops:
  0.0 57.0 %butterfly.1 = bf16[64,16384]{1,0:T(8,128)(2,1)S(1)} custom-call(bf16[64,16384]{1,0:T(8,128)(2,1)} %refs_0_.1, bf16[64,64,256]{2,1,0:T(8,128)(2,1)} %refs_1_.1, bf16[64,6,64,128]{3,2,1,0:T(8,128)(2,1)} %refs_2_.1, bf16[64,3,64,128]{3,2,1,0:T(8,128)(2,1)} %refs_3_.1, bf16[64,4,64,128]{3,2,1,0:T(8,128)(2,1)} %refs_4_.1, bf16[64,64,256]{2,1,0:T(8,128)(2,1)} %refs_5_.1), custom_call_target="tpu_custom_call" | custom-call | tf_op jit(solution)/shard_map/butterfly/pallas_call | solution.py:329
  57.1 1.3 %copy.8 = bf16[64,16384]{1,0:T(8,128)(2,1)} copy(bf16[64,16384]{1,0:T(8,128)(2,1)S(1)} %butterfly.1) | data formatting | bytes 4194304

commit v7 on v6

--- a/solution.py
+++ b/solution.py
@@ -13,7 +13,7 @@
 FARN = 8
 DIRECT = 7
 GROUP = 1
-DELAYS = (4, 5, 6, 5, 6, 5, 6)
+DELAYS = (5, 5, 6, 5, 6, 5, 6)
 CHUNKS = 4
 BLOCKS = ((10, 9), (8, 7, 6, 5), (4, 3, 2, 1, 0))
 UNROLL = 32

time: 58.5 us -> 58.4 us (level)
  no operation moved by 1% of the time
where the time goes in v7:
time: 58.4 us; the launch traced here: 58.3 us
  Pallas kernels  56.9 us (97%)
  local copies, waits for them, and re-layouts  1.32 us (2%)
    pallas_call x1, Pallas kernels, body(): pl.pallas_call(functools.partial(kernel, lo_levels, hi_levels), out_shape...  56.9 us
    unnamed x1, local copies, waits for them, and re-layouts  1.32 us

profile of v7, /device:TPU:0, one launch (start us, length us, event | category | flops | bytes accessed | tf_op | source)
XLA Modules:
  0.0 58.3 jit_solution(12574741549116944465)
XLA Ops:
  0.0 56.9 %butterfly.1 = bf16[64,16384]{1,0:T(8,128)(2,1)S(1)} custom-call(bf16[64,16384]{1,0:T(8,128)(2,1)} %refs_0_.1, bf16[64,64,256]{2,1,0:T(8,128)(2,1)} %refs_1_.1, bf16[64,6,64,128]{3,2,1,0:T(8,128)(2,1)} %refs_2_.1, bf16[64,3,64,128]{3,2,1,0:T(8,128)(2,1)} %refs_3_.1, bf16[64,4,64,128]{3,2,1,0:T(8,128)(2,1)} %refs_4_.1, bf16[64,64,256]{2,1,0:T(8,128)(2,1)} %refs_5_.1), custom_call_target="tpu_custom_call" | custom-call | tf_op jit(solution)/shard_map/butterfly/pallas_call | solution.py:329
  56.9 1.3 %copy.8 = bf16[64,16384]{1,0:T(8,128)(2,1)} copy(bf16[64,16384]{1,0:T(8,128)(2,1)S(1)} %butterfly.1) | data formatting | bytes 4194304
